TPU v7x, 1024 devices: a whole 8x8x8 slice. The times are simulated.
1024 devices in a mesh: own: 64 (over z, x), rep: 16 (over y, core).
Axes of the slice: x: 8, y: 8, z: 8, core: 2. Of those that a mesh axis runs over, the one named last changes fastest.
Arguments:
- features: bfloat16 [4096, 128, 512], P(('own', 'rep')), may hold values from -6 to 6
- adj_cols: int32 [4096, 4], P(('own', 'rep')), may hold values from 0 to 4095, as said below
- adj_counts: int32 [4096], P(('own', 'rep')), may hold values from 2 to 4, as said below
- adj_vals: bfloat16 [4096, 4, 128, 128], P(('own', 'rep')), may hold values from -0.3125 to 0.3125
- weight: bfloat16 [512, 512], replicated, may hold values from -0.25 to 0.25
- cotangent: bfloat16 [4096, 128, 512], P(('own', 'rep')), may hold values from -6 to 6
Outputs:
- output: bfloat16 [4096, 128, 512], P(('own', 'rep'))
- grad_features: float32 [4096, 128, 512], P(('own', 'rep'))
- grad_weight: float32 [512, 512], replicated
Inputs may be any that keep to these rules, and one draw needn't show every extreme that they name: `adj_cols`: the block columns of a row's slots are distinct and lie within 2 blocks of the row, counted cyclically over the 4096 blocks; slot 0 names the row itself, slot 1 the block before it for even rows and the block after it for odd rows. `adj_counts`: loads differ between devices; 4 is reached in every draw.
All inputs are finite; a program needn't handle non-finite values.
Results may differ from a plain program's by a relative error of at most 0.0054.
Values may be sent and summed in bfloat16 or wider, within the bound.
A program may use at most 32 MiB of HBM per device.

v0:
```python
import jax
import jax.numpy as jnp
from jax import lax
from jax.sharding import PartitionSpec as P

REACH = 2


def extended_2(cells, sides, width):
    for axis, dim in sides:
        count = lax.axis_size(axis)
        head = lax.slice_in_dim(cells, 0, width, axis=dim)
        tail = lax.slice_in_dim(cells, cells.shape[dim] - width, cells.shape[dim], axis=dim)
        cells = jnp.concatenate(
            [
                lax.ppermute(tail, axis, [(i, (i + 1) % count) for i in range(count)]),
                cells,
                lax.ppermute(head, axis, [((i + 1) % count, i) for i in range(count)]),
            ],
            axis=dim,
        )
    return cells


def per_device(features, adj_cols, adj_counts, adj_vals, weight, cotangent):
    row_blocks = features.shape[0]
    feature_width = features.shape[2]
    slot_count = adj_cols.shape[1]
    total_blocks = lax.axis_size(("own", "rep")) * row_blocks
    leading_row = lax.axis_index(("own", "rep")) * row_blocks
    local_rows = jnp.arange(row_blocks, dtype=jnp.int32)
    offsets = (
        jnp.remainder(adj_cols - (leading_row + local_rows)[:, None] + REACH, total_blocks) - REACH
    )
    positions = local_rows[:, None] + REACH + offsets
    slot_ids = jnp.arange(slot_count, dtype=jnp.int32)
    used_mask = slot_ids[None, :] < adj_counts[:, None]
    masked = jnp.where(used_mask[:, :, None, None], adj_vals, jnp.zeros((), adj_vals.dtype))
    extended = extended_2(features, ((("own", "rep"), 0),), REACH)
    chosen = jnp.take(extended, positions, axis=0)
    summed = jnp.einsum("nkab,nkbf->naf", masked, chosen, preferred_element_type=jnp.float32)
    hidden = summed.astype(jnp.bfloat16)
    flat_rows = hidden.reshape(-1, feature_width)
    preact = jnp.dot(flat_rows, weight, preferred_element_type=jnp.float32)
    output = jax.nn.silu(preact).astype(jnp.bfloat16).reshape(hidden.shape)
    sigmoid_pre = jax.nn.sigmoid(preact)
    slope = sigmoid_pre * (1.0 + preact * (1.0 - sigmoid_pre))
    grad_pre = (cotangent.reshape(-1, feature_width).astype(jnp.float32) * slope).astype(
        jnp.bfloat16
    )
    grad_hidden = (
        lax.dot_general(
            grad_pre, weight, (((1,), (1,)), ((), ())), preferred_element_type=jnp.float32
        )
        .astype(jnp.bfloat16)
        .reshape(hidden.shape)
    )
    local_weight = lax.dot_general(
        flat_rows, grad_pre, (((0,), (0,)), ((), ())), preferred_element_type=jnp.float32
    )
    grad_weight = lax.psum(local_weight, ("own", "rep"))
    extent = row_blocks + 2 * REACH
    target_positions = jnp.arange(extent, dtype=jnp.int32)
    selection_mask = (positions[:, :, None] == target_positions[None, None, :]).astype(jnp.float32)
    message_terms = jnp.einsum(
        "nkab,naf->nkbf", masked, grad_hidden, preferred_element_type=jnp.float32
    )
    positioned_rows = jnp.einsum(
        "mhx,mhza->xza", selection_mask, message_terms, precision=lax.Precision.HIGHEST
    )
    rims = jnp.concatenate([positioned_rows[:REACH], positioned_rows[row_blocks + REACH :]], axis=0)
    arrived = extended_2(rims.astype(jnp.bfloat16), ((("own", "rep"), 0),), REACH).astype(
        rims.dtype
    )
    inner = positioned_rows[REACH : REACH + row_blocks]
    inner = inner.at[:REACH].add(arrived[:REACH])
    inner = inner.at[row_blocks - REACH :].add(arrived[3 * REACH :])
    return (output, inner, grad_weight)


def solution(mesh):
    return jax.shard_map(
        per_device,
        mesh=mesh,
        in_specs=(
            P(("own", "rep"), None, None),
            P(("own", "rep"), None),
            P(("own", "rep")),
            P(("own", "rep"), None, None, None),
            P(),
            P(("own", "rep"), None, None),
        ),
        out_specs=(P(("own", "rep"), None, None), P(("own", "rep"), None, None), P()),
        check_vma=False,
    )
```

profile of v0, /device:TPU:1, one launch (start us, length us, event | category | flops | bytes accessed | tf_op | source)
XLA Modules:
  0.0 354.3 jit_solution(17920700461850773592)
XLA Ops:
  7.2 0.0 copy-start
  7.2 0.0 all-reduce.2.cloned.1.call-start
  7.2 1.1 fusion.32
  8.3 4.7 %collective-permute-start = (bf16[2,128,512]{2,1,0:T(8,128)(2,1)S(1)}, bf16[2,128,512]{2,1,0:T(8,128)(2,1)S(1)}, u32[]{:S(2)}, u32[]{:S(2)}) collective-permute-start(bf16[2,128,512]{2,1,0:T(8,128)(2,1)S(1)} %get-tuple-element.36), channel_id=1, source_target_pairs={{0,1},{1,2},{2,3},{3,4},{4,5},{5,6},{6,7},{7,8},{8,9},{9,10},{10,1... | collective-permute-start | bytes 786440 | tf_op jit(solution)/shard_map/ppermute | solution.py:16
  13.1 13.3 %collective-permute-start.1 = (bf16[2,128,512]{2,1,0:T(8,128)(2,1)S(1)}, bf16[2,128,512]{2,1,0:T(8,128)(2,1)S(1)}, u32[]{:S(2)}, u32[]{:S(2)}) collective-permute-start(bf16[2,128,512]{2,1,0:T(8,128)(2,1)S(1)} %get-tuple-element.37), channel_id=1, source_target_pairs={{1,0},{2,1},{3,2},{4,3},{5,4},{6,5},{7,6},{8,7},{9,8},{10,9},{11,1... | collective-permute-start | bytes 786440 | tf_op jit(solution)/shard_map/ppermute | solution.py:18
  26.4 0.8 compare_and_fusion
  27.1 0.1 reshape.120
  27.2 0.1 copy.9
  27.3 0.7 iota_compare_fusion.1
  28.1 0.0 collective-permute-done
  28.1 0.0 collective-permute-done.1
  28.1 1.2 pad_maximum_fusion
  29.2 0.0 copy-start.1
  29.2 2.0 gather_fusion
  31.2 0.0 copy-done.1
  31.3 0.0 copy-start.2
  31.3 2.2 fusion.11
  33.5 0.0 copy-done
  33.5 0.0 copy-done.2
  33.5 1.6 fusion.14
  35.1 0.5 convolution_convert_fusion
  35.6 0.9 fusion.18
  36.5 6.1 %fusion.33 = (bf16[8,128,512]{2,0,1:T(8,128)(2,1)S(1)}, f32[8,128,512]{2,0,1:T(8,128)S(1)}) fusion(f32[4,4,128,512]{3,2,1,0:T(8,128)S(1)} %fusion.18, s32[4,4]{0,1:T(4,128)S(1)} %copy.9), kind=kOutput, calls=%fused_computation.47 | convolution fusion | flops 101187712 | bytes 7340096 | tf_op jit(solution)/shard_map/mhx,mhza->xza/dot_general | solution.py:68
  42.6 0.3 fusion.31
  43.0 1.9 collective-permute-start.2
  44.9 12.4 %collective-permute-start.3 = (bf16[2,128,512]{2,0,1:T(2,128)(2,1)S(1)}, bf16[2,128,512]{2,0,1:T(2,128)(2,1)}, u32[]{:S(2)}, u32[]{:S(2)}) collective-permute-start(bf16[2,128,512]{2,0,1:T(2,128)(2,1)S(1)} %get-tuple-element.33), channel_id=1, source_target_pairs={{1,0},{2,1},{3,2},{4,3},{5,4},{6,5},{7,6},{8,7},{9,8},{10,9},{11,1... | collective-permute-start | bytes 786440 | tf_op jit(solution)/shard_map/ppermute | solution.py:18
  57.3 1.4 fusion.34
  58.8 0.0 all-reduce.2.cloned.1.call-update
  58.8 0.3 slice.85
  59.1 0.0 collective-permute-done.2
  59.1 0.0 collective-permute-done.3
  59.1 2.5 fusion.17
  61.5 2.5 fusion.16
  64.1 1.3 copy.10
  65.4 279.8 %all-reduce.2.cloned.1.call-done = f32[512,512]{1,0:T(8,128)} async-done(((f32[512,512]{1,0:T(8,128)}), f32[512,512]{1,0:T(8,128)}) %all-reduce.2.cloned.1.call-update) | async-done | bytes 1048592 | tf_op jit(solution)/shard_map/psum | solution.py:61
  345.2 2.3 copy.24
  (3 shorter events, 0.0 us)
Async XLA Ops:
  7.2 26.3 %copy-start = (bf16[512,512]{1,0:T(8,128)(2,1)S(1)}, bf16[512,512]{1,0:T(8,128)(2,1)}, u32[]{:S(2)}) copy-start(bf16[512,512]{1,0:T(8,128)(2,1)} %param.14) | copy-start | bytes 1572868
  7.2 338.0 %all-reduce.2.cloned.1.call-start = ((), (), s32[]{:S(2)}) async-start(), calls=%async_computation | async-start | bytes 2097152 | tf_op jit(solution)/shard_map/psum | solution.py:61
  8.3 19.7 %collective-permute-start = (bf16[2,128,512]{2,1,0:T(8,128)(2,1)S(1)}, bf16[2,128,512]{2,1,0:T(8,128)(2,1)S(1)}, u32[]{:S(2)}, u32[]{:S(2)}) collective-permute-start(bf16[2,128,512]{2,1,0:T(8,128)(2,1)S(1)} %get-tuple-element.36), channel_id=1, source_target_pairs={{0,1},{1,2},{2,3},{3,4},{4,5},{5,6},{6,7},{7,8},{8,9},{9,10},{10,1... | collective-permute-start | bytes 786440 | tf_op jit(solution)/shard_map/ppermute | solution.py:16
  13.1 15.0 %collective-permute-start.1 = (bf16[2,128,512]{2,1,0:T(8,128)(2,1)S(1)}, bf16[2,128,512]{2,1,0:T(8,128)(2,1)S(1)}, u32[]{:S(2)}, u32[]{:S(2)}) collective-permute-start(bf16[2,128,512]{2,1,0:T(8,128)(2,1)S(1)} %get-tuple-element.37), channel_id=1, source_target_pairs={{1,0},{2,1},{3,2},{4,3},{5,4},{6,5},{7,6},{8,7},{9,8},{10,9},{11,1... | collective-permute-start | bytes 786440 | tf_op jit(solution)/shard_map/ppermute | solution.py:18
  29.2 2.0 copy-start.1
  31.3 2.2 copy-start.2
  43.0 16.1 %collective-permute-start.2 = (bf16[2,128,512]{2,0,1:T(2,128)(2,1)S(1)}, bf16[2,128,512]{2,0,1:T(2,128)(2,1)S(1)}, u32[]{:S(2)}, u32[]{:S(2)}) collective-permute-start(bf16[2,128,512]{2,0,1:T(2,128)(2,1)S(1)} %get-tuple-element.32), channel_id=1, source_target_pairs={{0,1},{1,2},{2,3},{3,4},{4,5},{5,6},{6,7},{7,8},{8,9},{9,10},{10,1... | collective-permute-start | bytes 786440 | tf_op jit(solution)/shard_map/ppermute | solution.py:16
  44.9 14.2 %collective-permute-start.3 = (bf16[2,128,512]{2,0,1:T(2,128)(2,1)S(1)}, bf16[2,128,512]{2,0,1:T(2,128)(2,1)}, u32[]{:S(2)}, u32[]{:S(2)}) collective-permute-start(bf16[2,128,512]{2,0,1:T(2,128)(2,1)S(1)} %get-tuple-element.33), channel_id=1, source_target_pairs={{1,0},{2,1},{3,2},{4,3},{5,4},{6,5},{7,6},{8,7},{9,8},{10,9},{11,1... | collective-permute-start | bytes 786440 | tf_op jit(solution)/shard_map/ppermute | solution.py:18
Sparse Core Ops, SparseCore 0:
  58.9 286.2 all-reduce.1
where the time goes:
time: 355 us; the launch traced here: 354 us
  waiting for transfers between devices  280 us (79%)
  starting transfers between devices  32.4 us (9%)
  between operations  14.2 us (4%)
  matrix products  12.7 us (4%)
  other arithmetic  7.66 us (2%)
  local copies, waits for them, and re-layouts  7.48 us (2%)
    psum x1, waiting for transfers between devices, per_device(): grad_weight = lax.psum(local_weight, ('own', 'rep'))  280 us
    ppermute x2, starting transfers between devices, extended_2(): lax.ppermute(head, axis, [((i + 1) % count, i) for i in range(count)])  25.7 us
  transfers between devices with their start and end apart: 5, of which 1 were waited for; matrix products, arithmetic and copies ran while one was open for 3% of the time, Pallas kernels for 0%

commit v1 on v0

v1 whole, which is shorter than its diff:
```python
import functools

import jax
import jax.numpy as jnp
from jax import lax
from jax.experimental import pallas as pl
from jax.experimental.pallas import tpu as pltpu
from jax.sharding import PartitionSpec as P

MESH = pl.DeviceIdType.MESH
F32 = jnp.float32
BF16 = jnp.bfloat16
REACH = 2
BLK = 128
PIECES = 2
ORDERS = ((2, 1, 0), (1, 0, 2), (0, 2, 1))


def dot(a, b, dims=((1,), (0,))):
    return lax.dot_general(a, b, (dims, ((), ())), preferred_element_type=F32)


def main_kernel(
    n, total_blocks,
    cols_h, counts_h, feat, vals, wgt, cot,
    out, gf, fa, fb, fc,
    cols, counts, ext, vals_v, w_v, cot_v, band, hid, grad_pre, hid_t, acc, own_half,
    core_out, core_in, rim_out, rim_in,
    sa, sb, sc, ra, rb, rc, ta, tb, tc, ua, ub, uc,
    load_sem, halo_send, halo_recv, rim_send, rim_recv, core_send, core_recv,
    step_send, step_recv, gather_send, gather_recv, fwd_send, fwd_recv,
):
    own = lax.axis_index("own")
    rep = lax.axis_index("rep")
    core = rep % 2
    place = (own // n, own % n, rep // 2)
    me = own * (2 * n) + rep
    count = n * n * n * 2

    def device(z, x, y, c):
        return {"own": z * n + x, "rep": y * 2 + c}

    def peer(axis, value):
        p = list(place)
        p[axis] = value
        return device(*p, core)

    def at_index(i):
        return {"own": i // (2 * n), "rep": i % (2 * n)}

    right = at_index((me + 1) % count)
    left = at_index((me + count - 1) % count)
    partner = device(*place, 1 - core)
    hops = sorted(range(1, n), key=lambda d: -min(d, n - d))

    loads = [
        pltpu.make_async_copy(feat, ext.at[pl.ds(256, 512)], load_sem.at[0]),
        pltpu.make_async_copy(vals, vals_v, load_sem.at[1]),
        pltpu.make_async_copy(wgt, w_v, load_sem.at[2]),
        pltpu.make_async_copy(cot, cot_v, load_sem.at[3]),
        pltpu.make_async_copy(cols_h, cols, load_sem.at[4]),
        pltpu.make_async_copy(counts_h, counts, load_sem.at[5]),
    ]
    for copy in loads:
        copy.start()

    barrier = pltpu.get_barrier_semaphore()
    for axis in range(3):
        for d in hops:
            pl.semaphore_signal(
                barrier, inc=1, device_id=peer(axis, (place[axis] + d) % n), device_id_type=MESH
            )
    pl.semaphore_signal(barrier, inc=1, device_id=left, device_id_type=MESH)
    pl.semaphore_signal(barrier, inc=1, device_id=right, device_id_type=MESH)

    row0 = me * 4
    loads[4].wait()
    loads[5].wait()
    loads[1].wait()
    for r in range(4):
        h, q = divmod(r, 2)
        rows = slice(q * BLK, (q + 1) * BLK)
        beside = -1 if q == 0 else 1
        third = counts[r] > 2
        fourth = counts[r] > 3
        c2, c3 = cols[r, 2], cols[r, 3]
        v2, v3 = vals_v[r * 4 + 2], vals_v[r * 4 + 3]
        for e in range(6):
            o = e - q - REACH
            if o == 0:
                block = vals_v[r * 4]
            elif o == beside:
                block = vals_v[r * 4 + 1]
            elif -REACH <= o <= REACH:
                name = (row0 + r + o + total_blocks) % total_blocks
                use2 = jnp.logical_and(third, c2 == name).astype(F32).astype(BF16)
                use3 = jnp.logical_and(fourth, c3 == name).astype(F32).astype(BF16)
                block = v2 * use2 + v3 * use3
            else:
                block = jnp.zeros((BLK, BLK), BF16)
            band[h, rows, e * BLK : (e + 1) * BLK] = block

    loads[0].wait()
    hid[0:256, :] = dot(band[0, :, 256:768], ext[256:768, :])
    hid[256:512, :] = dot(band[1, :, 0:512], ext[256:768, :])

    pl.semaphore_wait(barrier, 3 * (n - 1) + 2)

    send_right = pltpu.make_async_remote_copy(
        src_ref=ext.at[pl.ds(512, 256)], dst_ref=ext.at[pl.ds(0, 256)],
        send_sem=halo_send.at[0], recv_sem=halo_recv.at[0],
        device_id=right, device_id_type=MESH,
    )
    send_left = pltpu.make_async_remote_copy(
        src_ref=ext.at[pl.ds(256, 256)], dst_ref=ext.at[pl.ds(768, 256)],
        send_sem=halo_send.at[1], recv_sem=halo_recv.at[1],
        device_id=left, device_id_type=MESH,
    )
    send_right.start()
    send_left.start()
    loads[2].wait()
    loads[3].wait()

    def forward(h):
        rows = pl.ds(pl.multiple_of(256 * h, 256), 256)
        rim_cols = pl.ds(pl.multiple_of(512 * h, 512), 256)
        halo_rows = pl.ds(pl.multiple_of(768 * h, 256), 256)
        hidden = (hid[rows, :] + dot(band[h, :, rim_cols], ext[halo_rows, :])).astype(BF16)
        hid_t[...] = hidden.T
        preact = dot(hidden, w_v[...])
        sig = 1.0 / (1.0 + jnp.exp(-preact))
        out[rows, :] = (preact * sig).astype(BF16)
        slope = sig * (1.0 + preact * (1.0 - sig))
        grad_pre[rows, :] = (cot_v[rows, :].astype(F32) * slope).astype(BF16)

    def rim(h):
        return pltpu.make_async_remote_copy(
            src_ref=rim_out.at[h], dst_ref=rim_in.at[1 - h],
            send_sem=rim_send.at[h], recv_sem=rim_recv.at[1 - h],
            device_id=at_index((me + count - 1 + 2 * h) % count), device_id_type=MESH,
        )

    def backward(h, first):
        rows = pl.ds(pl.multiple_of(256 * h, 256), 256)
        rim_cols = pl.ds(pl.multiple_of(512 * h, 512), 256)
        inner_cols = pl.ds(pl.multiple_of(256 * (1 - h), 256), 512)
        grad_hidden = dot(grad_pre[rows, :], w_v[...], ((1,), (1,))).astype(BF16)
        rim_out[h] = dot(band[h, :, rim_cols], grad_hidden, ((0,), (0,))).astype(BF16)
        rim(h).start()
        inner = dot(band[h, :, inner_cols], grad_hidden, ((0,), (0,)))
        if first:
            gf[...] = inner
        else:
            gf[...] += inner

    near, far = 1 - core, core
    pltpu.make_async_remote_copy(
        src_ref=ext.at[pl.ds(256, 256)], dst_ref=ext.at[pl.ds(pl.multiple_of(768 * near, 256), 256)],
        send_sem=halo_send.at[0], recv_sem=halo_recv.at[near],
        device_id=partner, device_id_type=MESH,
    ).wait_recv()
    forward(near)
    acc[...] = dot(hid_t[...], grad_pre[pl.ds(pl.multiple_of(256 * near, 256), 256), :])
    backward(near, True)
    pltpu.make_async_remote_copy(
        src_ref=ext.at[pl.ds(256, 256)], dst_ref=ext.at[pl.ds(pl.multiple_of(768 * far, 256), 256)],
        send_sem=halo_send.at[0], recv_sem=halo_recv.at[far],
        device_id=partner, device_id_type=MESH,
    ).wait_recv()
    forward(far)

    far_rows = pl.ds(pl.multiple_of(256 * far, 256), 256)
    size = 256 // PIECES
    core_copies = []
    for q in range(PIECES):
        here = pl.ds(pl.multiple_of(256 * (1 - core) + size * q, size), size)
        core_out[q] = (acc[here, :] + dot(hid_t[here, :], grad_pre[far_rows, :])).astype(BF16)
        copy = pltpu.make_async_remote_copy(
            src_ref=core_out.at[q], dst_ref=core_in.at[q],
            send_sem=core_send.at[q], recv_sem=core_recv.at[q],
            device_id=partner, device_id_type=MESH,
        )
        copy.start()
        core_copies.append(copy)
    mine = pl.ds(pl.multiple_of(256 * core, 256), 256)
    own_half[...] = acc[mine, :] + dot(hid_t[mine, :], grad_pre[far_rows, :])

    width = 256 // n
    low = width // 2
    for q in range(PIECES):
        core_copies[q].wait_recv()
        chip = (own_half[size * q : size * (q + 1), :] + core_in[q].astype(F32)).astype(BF16)
        for i in range(n // PIECES):
            k = q * (n // PIECES) + i
            sa[k] = chip[width * i : width * i + low, 0:384]
            sb[k] = chip[width * i + low : width * (i + 1), 0:384]
            sc[k] = chip[width * i : width * (i + 1), 384:512]

    parts = ((sa, ra, ta, ua, fa), (sb, rb, tb, ub, fb), (sc, rc, tc, uc, fc))

    def send(src, dst, part, step, axis, value):
        pltpu.make_async_remote_copy(
            src_ref=src, dst_ref=dst, send_sem=step_send.at[part, step], recv_sem=step_recv.at[part, step],
            device_id=peer(axis, value), device_id_type=MESH,
        ).start()

    def arrived(buf, part, step):
        whole = buf.at[pl.ds(0, n - 1)]
        pltpu.make_async_remote_copy(
            src_ref=whole, dst_ref=whole, send_sem=step_send.at[part, step], recv_sem=step_recv.at[part, step],
            device_id=partner, device_id_type=MESH,
        ).wait_recv()

    def summed(buf):
        total = buf[0].astype(F32)
        for i in range(1, n):
            total = total + buf[i].astype(F32)
        return total.astype(BF16)

    for d in hops:
        for p, (s, r, t, u, f) in enumerate(parts):
            axis = ORDERS[p][0]
            j = (place[axis] + d) % n
            send(s.at[j], r.at[place[axis]], p, 0, axis, j)
    for p, (s, r, t, u, f) in enumerate(parts):
        i = place[ORDERS[p][0]]
        r[i] = s[i]
    backward(far, False)

    for step in (1, 2):
        for p, part in enumerate(parts):
            axis = ORDERS[p][step]
            arrived(part[step], p, step - 1)
            part[step + 1][place[axis]] = summed(part[step])
        for d in hops:
            for p, part in enumerate(parts):
                axis = ORDERS[p][step]
                here = part[step + 1].at[place[axis]]
                send(here, here, p, step, axis, (place[axis] + d) % n)
        if step == 2:
            for h in range(2):
                pltpu.make_async_remote_copy(
                    src_ref=rim_out.at[h], dst_ref=rim_in.at[h],
                    send_sem=rim_send.at[h], recv_sem=rim_recv.at[h],
                    device_id=partner, device_id_type=MESH,
                ).wait_recv()
                gf[256 * h : 256 * (h + 1), :] += rim_in[h].astype(F32)

    for p, (s, r, t, u, f) in enumerate(parts):
        arrived(u, p, 2)
        f[core, place[ORDERS[p][0]]] = summed(u)

    def gather(p, f, target, slot):
        here = f.at[core, slot]
        axis = ORDERS[p][0]
        return pltpu.make_async_remote_copy(
            src_ref=here, dst_ref=here, send_sem=gather_send.at[p], recv_sem=gather_recv.at[p, slot],
            device_id=peer(axis, target), device_id_type=MESH,
        )

    def onward(p, f, slot):
        here = f.at[core, slot]
        return pltpu.make_async_remote_copy(
            src_ref=here, dst_ref=here, send_sem=fwd_send.at[p], recv_sem=fwd_recv.at[p],
            device_id=partner, device_id_type=MESH,
        )

    for d in hops:
        for p, part in enumerate(parts):
            i = place[ORDERS[p][0]]
            gather(p, part[4], (i + d) % n, i).start()
    for p, part in enumerate(parts):
        onward(p, part[4], place[ORDERS[p][0]]).start()
    for d in hops[::-1]:
        for p, part in enumerate(parts):
            i = place[ORDERS[p][0]]
            j = (i + d) % n
            gather(p, part[4], j, j).wait_recv()
            onward(p, part[4], j).start()

    send_right.wait_send()
    send_left.wait_send()
    for h in range(2):
        pltpu.make_async_remote_copy(
            src_ref=rim_out.at[h], dst_ref=rim_in.at[h],
            send_sem=rim_send.at[h], recv_sem=rim_recv.at[h],
            device_id=partner, device_id_type=MESH,
        ).wait_send()
    for copy in core_copies:
        copy.wait_send()
    for p, part in enumerate(parts):
        for step in range(3):
            whole = part[0].at[pl.ds(0, n - 1)]
            pltpu.make_async_remote_copy(
                src_ref=whole, dst_ref=whole, send_sem=step_send.at[p, step], recv_sem=step_recv.at[p, step],
                device_id=partner, device_id_type=MESH,
            ).wait_send()
        whole = part[4].at[core, pl.ds(0, n - 1)]
        pltpu.make_async_remote_copy(
            src_ref=whole, dst_ref=whole, send_sem=gather_send.at[p], recv_sem=fwd_recv.at[p],
            device_id=partner, device_id_type=MESH,
        ).wait_send()
        for_partner = part[4].at[core]
        from_partner = part[4].at[1 - core]
        pltpu.make_async_remote_copy(
            src_ref=for_partner, dst_ref=from_partner, send_sem=fwd_send.at[p], recv_sem=fwd_recv.at[p],
            device_id=partner, device_id_type=MESH,
        ).wait()


def write_kernel(n, out, gf, fa, fb, fc, out_r, gf_r, gw_r, gw, sems):
    copies = [
        pltpu.make_async_copy(out, out_r, sems.at[0]),
        pltpu.make_async_copy(gf, gf_r, sems.at[1]),
    ]
    for copy in copies:
        copy.start()
    width = 256 // n
    low = width // 2
    for c in range(2):
        for k in range(n):
            top = 256 * c + width * k
            gw[top : top + low, 0:384] = fa[c, k].astype(F32)
            gw[top + low : top + width, 0:384] = fb[c, k].astype(F32)
            gw[top : top + width, 384:512] = fc[c, k].astype(F32)
        rows = pl.ds(256 * c, 256)
        copy = pltpu.make_async_copy(gw.at[rows], gw_r.at[rows], sems.at[2 + c])
        copy.start()
        copies.append(copy)
    for copy in copies:
        copy.wait()


def per_device(n, features, adj_cols, adj_counts, adj_vals, weight, cotangent):
    width = 256 // n
    low = width // 2
    vmem = pl.BlockSpec(memory_space=pltpu.VMEM)
    smem = pl.BlockSpec(memory_space=pltpu.SMEM)
    anyw = pl.BlockSpec(memory_space=pl.ANY)
    hbm = pl.BlockSpec(memory_space=pltpu.HBM)
    shapes = ((n, low, 384), (n, low, 384), (n, width, 128))
    dma = pltpu.SemaphoreType.DMA
    steps = [pltpu.VMEM(s, BF16) for _ in range(4) for s in shapes]
    args = (
        adj_cols,
        adj_counts,
        features.reshape(512, 512),
        adj_vals.reshape(16, BLK, BLK),
        weight,
        cotangent.reshape(512, 512),
    )
    out, gf, fa, fb, fc = pl.pallas_call(
        functools.partial(main_kernel, n, 4 * 2 * n**3),
        out_shape=(
            pltpu.VMEM((512, 512), BF16),
            pltpu.VMEM((512, 512), F32),
            *[pltpu.VMEM((2,) + s, BF16) for s in shapes],
        ),
        in_specs=[hbm] * 6,
        out_specs=(vmem,) * 5,
        scratch_shapes=[
            pltpu.SMEM((4, 4), jnp.int32),
            pltpu.SMEM((4,), jnp.int32),
            pltpu.VMEM((1024, 512), BF16),
            pltpu.VMEM((16, BLK, BLK), BF16),
            pltpu.VMEM((512, 512), BF16),
            pltpu.VMEM((512, 512), BF16),
            pltpu.VMEM((2, 256, 768), BF16),
            pltpu.VMEM((512, 512), F32),
            pltpu.VMEM((512, 512), BF16),
            pltpu.VMEM((512, 256), BF16),
            pltpu.VMEM((512, 512), F32),
            pltpu.VMEM((256, 512), F32),
            pltpu.VMEM((PIECES, 256 // PIECES, 512), BF16),
            pltpu.VMEM((PIECES, 256 // PIECES, 512), BF16),
            pltpu.VMEM((2, 256, 512), BF16),
            pltpu.VMEM((2, 256, 512), BF16),
            *steps,
            dma((6,)), dma((2,)), dma((2,)), dma((2,)), dma((2,)), dma((PIECES,)), dma((PIECES,)),
            dma((3, 3)), dma((3, 3)), dma((3,)), dma((3, n)), dma((3,)), dma((3,)),
        ],
        compiler_params=pltpu.CompilerParams(
            collective_id=0, has_side_effects=True, vmem_limit_bytes=40 * 2**20
        ),
        name="layer",
    )(*[pltpu.with_memory_space_constraint(a, pltpu.HBM) for a in args])
    out, gf, gw = pl.pallas_call(
        functools.partial(write_kernel, n),
        out_shape=(
            jax.ShapeDtypeStruct((512, 512), BF16),
            jax.ShapeDtypeStruct((512, 512), F32),
            jax.ShapeDtypeStruct((512, 512), F32),
        ),
        in_specs=[vmem] * 5,
        out_specs=(anyw,) * 3,
        scratch_shapes=[pltpu.VMEM((512, 512), F32), dma((4,))],
        compiler_params=pltpu.CompilerParams(vmem_limit_bytes=16 * 2**20),
        name="write",
    )(out, gf, fa, fb, fc)
    return out.reshape(4, BLK, 512), gf.reshape(4, BLK, 512), gw


def solution(mesh):
    n = mesh.shape["rep"] // 2
    both = ("own", "rep")
    return jax.shard_map(
        functools.partial(per_device, n),
        mesh=mesh,
        in_specs=(
            P(both, None, None),
            P(both, None),
            P(both),
            P(both, None, None, None),
            P(),
            P(both, None, None),
        ),
        out_specs=(P(both, None, None), P(both, None, None), P()),
        check_vma=False,
    )
```

time: 355 us -> 57.3 us (0.16)
  waiting for transfers between devices: 280 us -> 0 us
  Pallas kernels: 0 us -> 56.5 us
  starting transfers between devices: 32.4 us -> 0 us
  between operations: 14.2 us -> 0.64 us
  matrix products: 12.7 us -> 0 us
  other arithmetic: 7.66 us -> 0 us
  local copies, waits for them, and re-layouts: 7.48 us -> 0 us
    psum x1 -> x0, waiting for transfers between devices: 280 us -> none  [per_device(): grad_weight = lax.psum(local_weight, ('own', 'rep'))]
    pallas_call x0 -> x2, Pallas kernels: none -> 56.5 us  [the longest x1 55 us: per_device(): pl.pallas_call(functools.partial(main_kernel, n, 4 * 2 * n ** 3), out_sha...]
    ppermute x4 -> x0, starting transfers between devices: 32.4 us -> none  [the longest x2 25.7 us: extended_2(): lax.ppermute(head, axis, [((i + 1) % count, i) for i in range(count)])]
    dot_general x6 -> x0, matrix products: 12.7 us -> none  [the longest x1 6.12 us: per_device(): jnp.einsum('mhx,mhza->xza', selection_mask, message_terms, precision=lax....]
    scatter-add x2 -> x0, other arithmetic: 4.98 us -> none  [the longest x1 2.52 us: per_device(): inner = inner.at[row_blocks - REACH:].add(arrived[3 * REACH:])]
    unnamed x8 -> x0, local copies, waits for them, and re-layouts: 3.57 us -> none
  transfers between devices with their start and end apart: 5 -> 0, of which waited for: 1 -> 0; matrix products, arithmetic and copies ran while one was open for 3% -> 0% of each run, Pallas kernels for 0% -> 0%
where the time goes in v1:
time: 57.3 us; the launch traced here: 57.1 us
  Pallas kernels  56.5 us (99%)
  between operations  0.64 us (1%)
    pallas_call x1, Pallas kernels, per_device(): pl.pallas_call(functools.partial(main_kernel, n, 4 * 2 * n ** 3), out_sha...  55 us
    pallas_call x1, Pallas kernels, per_device(): pl.pallas_call(functools.partial(write_kernel, n), out_shape=(jax.ShapeDt...  1.52 us

profile of v1, /device:TPU:1, one launch (start us, length us, event | category | flops | bytes accessed | tf_op | source)
XLA Modules:
  0.0 57.1 jit_solution(9566833093643390827)
XLA Ops:
  0.6 55.0 %layer.1 = (bf16[512,512]{1,0:T(8,128)(2,1)S(1)}, f32[512,512]{1,0:T(8,128)S(1)}, bf16[2,8,16,384]{3,2,1,0:T(8,128)(2,1)S(1)}, bf16[2,8,16,384]{3,2,1,0:T(8,128)(2,1)S(1)}, bf16[2,8,32,128]{3,2,1,0:T(8,128)(2,1)S(1)}) custom-call(s32[4,4]{1,0:T(4,128)} %cols_h.1, s32[4]{0:T(128)} %counts_h.1, bf16[512,512]{1,0:T(8,128)(2,1)} %bitcast.5, ...), custom_call_target="tpu_custom_call" | custom-call | tf_op jit(solution)/shard_map/layer/pallas_call | solution.py:352
  55.6 1.5 %write.1 = (bf16[512,512]{1,0:T(8,128)(2,1)}, f32[512,512]{1,0:T(8,128)}, f32[512,512]{1,0:T(8,128)}) custom-call(bf16[512,512]{1,0:T(8,128)(2,1)S(1)} %get-tuple-element.11.out, f32[512,512]{1,0:T(8,128)S(1)} %get-tuple-element.12.gf, bf16[2,8,16,384]{3,2,1,0:T(8,128)(2,1)S(1)} %get-tuple-element.13.fa, bf16[2,8,16,384]{3,2,1,0:T(8,128)(2,1)S(1)} %get-tuple-element.14.fb, ...), custom_call_target="tpu_custom_call" | custom-call | tf_op jit(solution)/shard_map/write/pallas_call | solution.py:387

commit v2 on v1

--- a/solution.py
+++ b/solution.py
@@ -13,7 +13,8 @@
 REACH = 2
 BLK = 128
 PIECES = 2
-ORDERS = ((2, 1, 0), (1, 0, 2), (0, 2, 1))
+FAR = 3
+ORDERS = ((1, 0, 2), (0, 2, 1), (2, 1, 0))
 
 
 def dot(a, b, dims=((1,), (0,))):
@@ -24,10 +25,10 @@
     n, total_blocks,
     cols_h, counts_h, feat, vals, wgt, cot,
     out, gf, fa, fb, fc,
-    cols, counts, ext, vals_v, w_v, cot_v, band, hid, grad_pre, hid_t, acc, own_half,
+    cols, counts, ext, vals_v, w_v, cot_v, band, hid, grad_hid, grad_pre, hid_t, acc, own_half,
     core_out, core_in, rim_out, rim_in,
     sa, sb, sc, ra, rb, rc, ta, tb, tc, ua, ub, uc,
-    load_sem, halo_send, halo_recv, rim_send, rim_recv, core_send, core_recv,
+    ready, load_sem, halo_send, halo_recv, rim_send, rim_recv, core_send, core_recv,
     step_send, step_recv, gather_send, gather_recv, fwd_send, fwd_recv,
 ):
     own = lax.axis_index("own")
@@ -61,17 +62,36 @@
         pltpu.make_async_copy(cols_h, cols, load_sem.at[4]),
         pltpu.make_async_copy(counts_h, counts, load_sem.at[5]),
     ]
+    barrier = pltpu.get_barrier_semaphore()
+    for neighbour in (left, right):
+        pl.semaphore_signal(barrier, inc=1, device_id=neighbour, device_id_type=MESH)
     for copy in loads:
         copy.start()
-
-    barrier = pltpu.get_barrier_semaphore()
-    for axis in range(3):
-        for d in hops:
-            pl.semaphore_signal(
-                barrier, inc=1, device_id=peer(axis, (place[axis] + d) % n), device_id_type=MESH
-            )
-    pl.semaphore_signal(barrier, inc=1, device_id=left, device_id_type=MESH)
-    pl.semaphore_signal(barrier, inc=1, device_id=right, device_id_type=MESH)
+    beside = [
+        (axis, d) for d in sorted({d for d in (1, 2, n - 2, n - 1) if 0 < d < n}) for axis in range(3)
+    ]
+    for axis, d in beside:
+        pl.semaphore_signal(
+            barrier, inc=1, device_id=peer(axis, (place[axis] + d) % n), device_id_type=MESH
+        )
+
+    loads[0].wait()
+    pl.semaphore_wait(barrier, len(beside) + 2)
+    def halo(h):
+        return pltpu.make_async_remote_copy(
+            src_ref=ext.at[pl.ds(pl.multiple_of(256 + 256 * h, 256), 256)],
+            dst_ref=ext.at[pl.ds(pl.multiple_of(768 * (1 - h), 256), 256)],
+            send_sem=halo_send.at[h], recv_sem=halo_recv.at[1 - h],
+            device_id=at_index((me + count - 1 + 2 * h) % count), device_id_type=MESH,
+        )
+
+    near, far = 1 - core, core
+    halo(far).start()
+    halo(near).start()
+    for axis, d in beside:
+        pl.semaphore_signal(
+            ready, inc=1, device_id=peer(axis, (place[axis] + d) % n), device_id_type=MESH
+        )
 
     row0 = me * 4
     loads[4].wait()
@@ -80,7 +100,7 @@
     for r in range(4):
         h, q = divmod(r, 2)
         rows = slice(q * BLK, (q + 1) * BLK)
-        beside = -1 if q == 0 else 1
+        by = -1 if q == 0 else 1
         third = counts[r] > 2
         fourth = counts[r] > 3
         c2, c3 = cols[r, 2], cols[r, 3]
@@ -89,7 +109,7 @@
             o = e - q - REACH
             if o == 0:
                 block = vals_v[r * 4]
-            elif o == beside:
+            elif o == by:
                 block = vals_v[r * 4 + 1]
             elif -REACH <= o <= REACH:
                 name = (row0 + r + o + total_blocks) % total_blocks
@@ -100,24 +120,8 @@
                 block = jnp.zeros((BLK, BLK), BF16)
             band[h, rows, e * BLK : (e + 1) * BLK] = block
 
-    loads[0].wait()
     hid[0:256, :] = dot(band[0, :, 256:768], ext[256:768, :])
     hid[256:512, :] = dot(band[1, :, 0:512], ext[256:768, :])
-
-    pl.semaphore_wait(barrier, 3 * (n - 1) + 2)
-
-    send_right = pltpu.make_async_remote_copy(
-        src_ref=ext.at[pl.ds(512, 256)], dst_ref=ext.at[pl.ds(0, 256)],
-        send_sem=halo_send.at[0], recv_sem=halo_recv.at[0],
-        device_id=right, device_id_type=MESH,
-    )
-    send_left = pltpu.make_async_remote_copy(
-        src_ref=ext.at[pl.ds(256, 256)], dst_ref=ext.at[pl.ds(768, 256)],
-        send_sem=halo_send.at[1], recv_sem=halo_recv.at[1],
-        device_id=left, device_id_type=MESH,
-    )
-    send_right.start()
-    send_left.start()
     loads[2].wait()
     loads[3].wait()
 
@@ -140,20 +144,22 @@
             device_id=at_index((me + count - 1 + 2 * h) % count), device_id_type=MESH,
         )
 
+    def send_rim(h):
+        rows = pl.ds(pl.multiple_of(256 * h, 256), 256)
+        rim_cols = pl.ds(pl.multiple_of(512 * h, 512), 256)
+        grad_hid[rows, :] = dot(grad_pre[rows, :], w_v[...], ((1,), (1,))).astype(BF16)
+        rim_out[h] = dot(band[h, :, rim_cols], grad_hid[rows, :], ((0,), (0,))).astype(BF16)
+        rim(h).start()
+
     def backward(h, first):
         rows = pl.ds(pl.multiple_of(256 * h, 256), 256)
-        rim_cols = pl.ds(pl.multiple_of(512 * h, 512), 256)
         inner_cols = pl.ds(pl.multiple_of(256 * (1 - h), 256), 512)
-        grad_hidden = dot(grad_pre[rows, :], w_v[...], ((1,), (1,))).astype(BF16)
-        rim_out[h] = dot(band[h, :, rim_cols], grad_hidden, ((0,), (0,))).astype(BF16)
-        rim(h).start()
-        inner = dot(band[h, :, inner_cols], grad_hidden, ((0,), (0,)))
+        inner = dot(band[h, :, inner_cols], grad_hid[rows, :], ((0,), (0,)))
         if first:
             gf[...] = inner
         else:
             gf[...] += inner
 
-    near, far = 1 - core, core
     pltpu.make_async_remote_copy(
         src_ref=ext.at[pl.ds(256, 256)], dst_ref=ext.at[pl.ds(pl.multiple_of(768 * near, 256), 256)],
         send_sem=halo_send.at[0], recv_sem=halo_recv.at[near],
@@ -161,13 +167,14 @@
     ).wait_recv()
     forward(near)
     acc[...] = dot(hid_t[...], grad_pre[pl.ds(pl.multiple_of(256 * near, 256), 256), :])
-    backward(near, True)
+    send_rim(near)
     pltpu.make_async_remote_copy(
         src_ref=ext.at[pl.ds(256, 256)], dst_ref=ext.at[pl.ds(pl.multiple_of(768 * far, 256), 256)],
         send_sem=halo_send.at[0], recv_sem=halo_recv.at[far],
         device_id=partner, device_id_type=MESH,
     ).wait_recv()
     forward(far)
+    send_rim(far)
 
     far_rows = pl.ds(pl.multiple_of(256 * far, 256), 256)
     size = 256 // PIECES
@@ -217,6 +224,7 @@
             total = total + buf[i].astype(F32)
         return total.astype(BF16)
 
+    pl.semaphore_wait(ready, len(beside))
     for d in hops:
         for p, (s, r, t, u, f) in enumerate(parts):
             axis = ORDERS[p][0]
@@ -225,19 +233,25 @@
     for p, (s, r, t, u, f) in enumerate(parts):
         i = place[ORDERS[p][0]]
         r[i] = s[i]
-    backward(far, False)
+    backward(far, True)
+
+    def spread(p, part, step, distances):
+        axis = ORDERS[p][step]
+        here = part[step + 1].at[place[axis]]
+        for d in distances:
+            send(here, here, p, step, axis, (place[axis] + d) % n)
 
     for step in (1, 2):
         for p, part in enumerate(parts):
             axis = ORDERS[p][step]
             arrived(part[step], p, step - 1)
             part[step + 1][place[axis]] = summed(part[step])
-        for d in hops:
-            for p, part in enumerate(parts):
-                axis = ORDERS[p][step]
-                here = part[step + 1].at[place[axis]]
-                send(here, here, p, step, axis, (place[axis] + d) % n)
-        if step == 2:
+            spread(p, part, step, hops[:FAR])
+        for p, part in enumerate(parts):
+            spread(p, part, step, hops[FAR:])
+        if step == 1:
+            backward(near, False)
+        else:
             for h in range(2):
                 pltpu.make_async_remote_copy(
                     src_ref=rim_out.at[h], dst_ref=rim_in.at[h],
@@ -246,10 +260,6 @@
                 ).wait_recv()
                 gf[256 * h : 256 * (h + 1), :] += rim_in[h].astype(F32)
 
-    for p, (s, r, t, u, f) in enumerate(parts):
-        arrived(u, p, 2)
-        f[core, place[ORDERS[p][0]]] = summed(u)
-
     def gather(p, f, target, slot):
         here = f.at[core, slot]
         axis = ORDERS[p][0]
@@ -265,9 +275,15 @@
             device_id=partner, device_id_type=MESH,
         )
 
-    for d in hops:
-        for p, part in enumerate(parts):
-            i = place[ORDERS[p][0]]
+    for p, part in enumerate(parts):
+        i = place[ORDERS[p][0]]
+        arrived(part[3], p, 2)
+        part[4][core, i] = summed(part[3])
+        for d in hops[:FAR]:
+            gather(p, part[4], (i + d) % n, i).start()
+    for p, part in enumerate(parts):
+        i = place[ORDERS[p][0]]
+        for d in hops[FAR:]:
             gather(p, part[4], (i + d) % n, i).start()
     for p, part in enumerate(parts):
         onward(p, part[4], place[ORDERS[p][0]]).start()
@@ -278,9 +294,8 @@
             gather(p, part[4], j, j).wait_recv()
             onward(p, part[4], j).start()
 
-    send_right.wait_send()
-    send_left.wait_send()
     for h in range(2):
+        halo(h).wait_send()
         pltpu.make_async_remote_copy(
             src_ref=rim_out.at[h], dst_ref=rim_in.at[h],
             send_sem=rim_send.at[h], recv_sem=rim_recv.at[h],
@@ -368,6 +383,7 @@
             pltpu.VMEM((2, 256, 768), BF16),
             pltpu.VMEM((512, 512), F32),
             pltpu.VMEM((512, 512), BF16),
+            pltpu.VMEM((512, 512), BF16),
             pltpu.VMEM((512, 256), BF16),
             pltpu.VMEM((512, 512), F32),
             pltpu.VMEM((256, 512), F32),
@@ -376,7 +392,7 @@
             pltpu.VMEM((2, 256, 512), BF16),
             pltpu.VMEM((2, 256, 512), BF16),
             *steps,
-            dma((6,)), dma((2,)), dma((2,)), dma((2,)), dma((2,)), dma((PIECES,)), dma((PIECES,)),
+            pltpu.SemaphoreType.REGULAR, dma((6,)), dma((2,)), dma((2,)), dma((2,)), dma((2,)), dma((PIECES,)), dma((PIECES,)),
             dma((3, 3)), dma((3, 3)), dma((3,)), dma((3, n)), dma((3,)), dma((3,)),
         ],
         compiler_params=pltpu.CompilerParams(

time: 57.3 us -> 55.9 us (0.976)
  Pallas kernels: 56.5 us -> 55.1 us
    pallas_call x1, Pallas kernels: 55 us -> 53.5 us  [per_device(): pl.pallas_call(functools.partial(main_kernel, n, 4 * 2 * n ** 3), out_sha...]
where the time goes in v2:
time: 55.9 us; the launch traced here: 55.7 us
  Pallas kernels  55.1 us (99%)
  between operations  0.64 us (1%)
    pallas_call x1, Pallas kernels, per_device(): pl.pallas_call(functools.partial(main_kernel, n, 4 * 2 * n ** 3), out_sha...  53.5 us
    pallas_call x1, Pallas kernels, per_device(): pl.pallas_call(functools.partial(write_kernel, n), out_shape=(jax.ShapeDt...  1.52 us

profile of v2, /device:TPU:1, one launch (start us, length us, event | category | flops | bytes accessed | tf_op | source)
XLA Modules:
  0.0 55.7 jit_solution(3615290071673182108)
XLA Ops:
  0.6 53.5 %layer.1 = (bf16[512,512]{1,0:T(8,128)(2,1)S(1)}, f32[512,512]{1,0:T(8,128)S(1)}, bf16[2,8,16,384]{3,2,1,0:T(8,128)(2,1)S(1)}, bf16[2,8,16,384]{3,2,1,0:T(8,128)(2,1)S(1)}, bf16[2,8,32,128]{3,2,1,0:T(8,128)(2,1)S(1)}) custom-call(s32[4,4]{1,0:T(4,128)} %cols_h.1, s32[4]{0:T(128)} %counts_h.1, bf16[512,512]{1,0:T(8,128)(2,1)} %bitcast.5, ...), custom_call_target="tpu_custom_call" | custom-call | tf_op jit(solution)/shard_map/layer/pallas_call | solution.py:367
  54.2 1.5 %write.1 = (bf16[512,512]{1,0:T(8,128)(2,1)}, f32[512,512]{1,0:T(8,128)}, f32[512,512]{1,0:T(8,128)}) custom-call(bf16[512,512]{1,0:T(8,128)(2,1)S(1)} %get-tuple-element.11.out, f32[512,512]{1,0:T(8,128)S(1)} %get-tuple-element.12.gf, bf16[2,8,16,384]{3,2,1,0:T(8,128)(2,1)S(1)} %get-tuple-element.13.fa, bf16[2,8,16,384]{3,2,1,0:T(8,128)(2,1)S(1)} %get-tuple-element.14.fb, ...), custom_call_target="tpu_custom_call" | custom-call | tf_op jit(solution)/shard_map/write/pallas_call | solution.py:403

commit v3 on v2

--- a/solution.py
+++ b/solution.py
@@ -67,9 +67,8 @@
         pl.semaphore_signal(barrier, inc=1, device_id=neighbour, device_id_type=MESH)
     for copy in loads:
         copy.start()
-    beside = [
-        (axis, d) for d in sorted({d for d in (1, 2, n - 2, n - 1) if 0 < d < n}) for axis in range(3)
-    ]
+    beside = [(axis, d) for d in sorted({1, n - 1}) for axis in range(3)]
+    second = [(axis, d) for d in sorted({d for d in (2, n - 2) if 0 < d < n}) for axis in range(3)]
     for axis, d in beside:
         pl.semaphore_signal(
             barrier, inc=1, device_id=peer(axis, (place[axis] + d) % n), device_id_type=MESH
@@ -90,7 +89,7 @@
     halo(near).start()
     for axis, d in beside:
         pl.semaphore_signal(
-            ready, inc=1, device_id=peer(axis, (place[axis] + d) % n), device_id_type=MESH
+            ready.at[0], inc=1, device_id=peer(axis, (place[axis] + d) % n), device_id_type=MESH
         )
 
     row0 = me * 4
@@ -168,6 +167,11 @@
     forward(near)
     acc[...] = dot(hid_t[...], grad_pre[pl.ds(pl.multiple_of(256 * near, 256), 256), :])
     send_rim(near)
+    pl.semaphore_wait(ready.at[0], len(beside))
+    for axis, d in second:
+        pl.semaphore_signal(
+            ready.at[1], inc=1, device_id=peer(axis, (place[axis] + d) % n), device_id_type=MESH
+        )
     pltpu.make_async_remote_copy(
         src_ref=ext.at[pl.ds(256, 256)], dst_ref=ext.at[pl.ds(pl.multiple_of(768 * far, 256), 256)],
         send_sem=halo_send.at[0], recv_sem=halo_recv.at[far],
@@ -224,7 +228,8 @@
             total = total + buf[i].astype(F32)
         return total.astype(BF16)
 
-    pl.semaphore_wait(ready, len(beside))
+    if second:
+        pl.semaphore_wait(ready.at[1], len(second))
     for d in hops:
         for p, (s, r, t, u, f) in enumerate(parts):
             axis = ORDERS[p][0]
@@ -392,7 +397,7 @@
             pltpu.VMEM((2, 256, 512), BF16),
             pltpu.VMEM((2, 256, 512), BF16),
             *steps,
-            pltpu.SemaphoreType.REGULAR, dma((6,)), dma((2,)), dma((2,)), dma((2,)), dma((2,)), dma((PIECES,)), dma((PIECES,)),
+            pltpu.SemaphoreType.REGULAR((2,)), dma((6,)), dma((2,)), dma((2,)), dma((2,)), dma((2,)), dma((PIECES,)), dma((PIECES,)),
             dma((3, 3)), dma((3, 3)), dma((3,)), dma((3, n)), dma((3,)), dma((3,)),
         ],
         compiler_params=pltpu.CompilerParams(

time: 55.9 us -> 55.7 us (level)
  no operation moved by 1% of the time
where the time goes in v3:
time: 55.7 us; the launch traced here: 55.5 us
  Pallas kernels  54.9 us (99%)
  between operations  0.64 us (1%)
    pallas_call x1, Pallas kernels, per_device(): pl.pallas_call(functools.partial(main_kernel, n, 4 * 2 * n ** 3), out_sha...  53.3 us
    pallas_call x1, Pallas kernels, per_device(): pl.pallas_call(functools.partial(write_kernel, n), out_shape=(jax.ShapeDt...  1.52 us

profile of v3, /device:TPU:1, one launch (start us, length us, event | category | flops | bytes accessed | tf_op | source)
XLA Modules:
  0.0 55.5 jit_solution(8182390990744905739)
XLA Ops:
  0.6 53.3 %layer.1 = (bf16[512,512]{1,0:T(8,128)(2,1)S(1)}, f32[512,512]{1,0:T(8,128)S(1)}, bf16[2,8,16,384]{3,2,1,0:T(8,128)(2,1)S(1)}, bf16[2,8,16,384]{3,2,1,0:T(8,128)(2,1)S(1)}, bf16[2,8,32,128]{3,2,1,0:T(8,128)(2,1)S(1)}) custom-call(s32[4,4]{1,0:T(4,128)} %cols_h.1, s32[4]{0:T(128)} %counts_h.1, bf16[512,512]{1,0:T(8,128)(2,1)} %bitcast.5, ...), custom_call_target="tpu_custom_call" | custom-call | tf_op jit(solution)/shard_map/layer/pallas_call | solution.py:372
  54.0 1.5 %write.1 = (bf16[512,512]{1,0:T(8,128)(2,1)}, f32[512,512]{1,0:T(8,128)}, f32[512,512]{1,0:T(8,128)}) custom-call(bf16[512,512]{1,0:T(8,128)(2,1)S(1)} %get-tuple-element.11.out, f32[512,512]{1,0:T(8,128)S(1)} %get-tuple-element.12.gf, bf16[2,8,16,384]{3,2,1,0:T(8,128)(2,1)S(1)} %get-tuple-element.13.fa, bf16[2,8,16,384]{3,2,1,0:T(8,128)(2,1)S(1)} %get-tuple-element.14.fb, ...), custom_call_target="tpu_custom_call" | custom-call | tf_op jit(solution)/shard_map/write/pallas_call | solution.py:408
